TPU v7x, 512 devices: a whole 4x8x8 slice. The times are simulated.
512 devices in a mesh: ctxlo: 16 (over x_hi, z), ctxhi: 32 (over y, x_lo, core).
Axes of the slice: x: 4 (x_hi: 2, x_lo: 2; x = x_hi * 2 + x_lo), y: 8, z: 8, core: 2. Of those that a mesh axis runs over, the one named last changes fastest.
Arguments:
- query_matrix: float32 [131072, 1536], P(('ctxhi', 'ctxlo')), may hold values from -6 to 6
- key_matrix: float32 [131072, 256], P(('ctxhi', 'ctxlo')), may hold values from -6 to 6
- value_matrix: float32 [131072, 256], P(('ctxhi', 'ctxlo')), may hold values from -24 to 24
- block_lists: int32 [1024, 15], P(('ctxhi', 'ctxlo')), may hold values from -1 to 1023, as said below
Outputs:
- attended: float32 [131072, 1536], P(('ctxhi', 'ctxlo'))
Inputs may be any that keep to these rules, and one draw needn't show every extreme that they name: `block_lists`: row q holds distinct key blocks, each one of q, q - 1, q - 2, q - 3 and q - 2**j for j >= 2, never below 0, always including q itself, in any order; the other slots hold -1.
All inputs are finite; a program needn't handle non-finite values.
Results may differ from a plain program's by a relative error of at most 0.0003.
Values sent between devices are 32-bit elements; how exact they have to be, the bound alone decides.
A program may use at most 64 MiB of HBM per device.

v0:
```python
import jax
import jax.numpy as jnp
from jax import lax
from jax.sharding import PartitionSpec as P

QUERY_HEADS = 12
KEY_VALUE_HEADS = 2
HEAD_FEATURES = 128
BLOCK_TOKENS = 128


def shifted(block, axis, distance):
    devices = range(lax.axis_size(axis))
    route = [((i - distance) % len(devices), i) for i in devices]
    return lax.ppermute(block, axis, route)


def shifted_2(block, axis, distance):
    devices = range(lax.axis_size(axis))
    route = [(i - distance, i) for i in devices if i - distance in devices]
    return lax.ppermute(block, axis, route)


def body(query_matrix, key_matrix, value_matrix, block_lists):
    per_device = query_matrix.shape[0] // BLOCK_TOKENS
    inner_size = lax.axis_size("ctxlo")
    outer_size = lax.axis_size("ctxhi")
    inner_index = lax.axis_index("ctxlo")
    outer_index = lax.axis_index("ctxhi")
    device_index = outer_index * inner_size + inner_index
    block_count = per_device * inner_size * outer_size
    distances = [0, 1, 2, 3] + [
        2**power_level for power_level in range(2, 40) if 2**power_level < block_count
    ]
    key_value = jnp.concatenate([key_matrix, value_matrix], axis=1)
    needed = sorted(
        {
            -((local_block - distance) // per_device)
            for distance in distances
            for local_block in range(per_device)
        }
        - {0}
    )
    shards = {0: key_value}
    for offset in needed:
        inner_step = offset % inner_size
        outer_hop = offset // inner_size
        inner_moved = shifted(key_value, "ctxlo", inner_step) if inner_step else key_value
        direct = shifted_2(inner_moved, "ctxhi", outer_hop) if outer_hop else inner_moved
        if inner_step:
            if outer_hop + 1 < outer_size:
                carried = shifted_2(inner_moved, "ctxhi", outer_hop + 1)
            else:
                carried = jnp.zeros_like(inner_moved)
            shards[offset] = jnp.where(inner_index >= inner_step, direct, carried)
        else:
            shards[offset] = direct
    group_width = QUERY_HEADS // KEY_VALUE_HEADS
    score_scale = HEAD_FEATURES ** (-0.5)
    distance_array = jnp.array(distances, jnp.int32)
    row_ids = lax.broadcasted_iota(jnp.int32, (BLOCK_TOKENS, 1, BLOCK_TOKENS), 0)
    col_ids = lax.broadcasted_iota(jnp.int32, (BLOCK_TOKENS, 1, BLOCK_TOKENS), 2)
    causal = col_ids <= row_ids
    outputs = []
    for local_block in range(per_device):
        query_block_index = device_index * per_device + local_block
        pieces = []
        for distance in distances:
            offset = -((local_block - distance) // per_device)
            row_start = (local_block - distance) % per_device * BLOCK_TOKENS
            pieces.append(shards[offset][row_start : row_start + BLOCK_TOKENS])
        collected_rows = jnp.concatenate(pieces, axis=0)
        targets = query_block_index - distance_array
        listed = jnp.any(block_lists[local_block][None, :] == targets[:, None], axis=1) & (
            targets >= 0
        )
        allowed = listed[None, :, None] & ((distance_array[None, :, None] > 0) | causal)
        allowed = allowed.reshape(BLOCK_TOKENS, len(distances) * BLOCK_TOKENS)
        query_block_rows = query_matrix[
            local_block * BLOCK_TOKENS : (local_block + 1) * BLOCK_TOKENS
        ]
        head_outputs = []
        for head_cluster in range(KEY_VALUE_HEADS):
            query_portion = query_block_rows[
                :,
                head_cluster
                * group_width
                * HEAD_FEATURES : (head_cluster + 1)
                * group_width
                * HEAD_FEATURES,
            ].reshape(BLOCK_TOKENS, group_width, HEAD_FEATURES)
            key_portion = collected_rows[
                :, head_cluster * HEAD_FEATURES : (head_cluster + 1) * HEAD_FEATURES
            ]
            value_portion = collected_rows[
                :,
                (KEY_VALUE_HEADS + head_cluster)
                * HEAD_FEATURES : (KEY_VALUE_HEADS + head_cluster + 1)
                * HEAD_FEATURES,
            ]
            scores = (
                jnp.einsum(
                    "rgd,kd->grk", query_portion, key_portion, precision=lax.Precision.HIGHEST
                )
                * score_scale
            )
            scores = jnp.where(allowed[None], scores, -jnp.inf)
            row_max = jnp.max(scores, axis=2, keepdims=True)
            weights = jnp.exp(scores - row_max)
            denominator = jnp.sum(weights, axis=2)
            weighted = jnp.einsum(
                "grk,kd->rgd", weights, value_portion, precision=lax.Precision.HIGHEST
            )
            head_outputs.append(
                (weighted / jnp.transpose(denominator)[:, :, None]).reshape(
                    BLOCK_TOKENS, group_width * HEAD_FEATURES
                )
            )
        outputs.append(jnp.concatenate(head_outputs, axis=1))
    return jnp.concatenate(outputs, axis=0)


def solution(mesh):
    in_specs = (
        P(("ctxhi", "ctxlo"), None),
        P(("ctxhi", "ctxlo"), None),
        P(("ctxhi", "ctxlo"), None),
        P(("ctxhi", "ctxlo"), None),
    )
    out_specs = P(("ctxhi", "ctxlo"), None)
    return jax.shard_map(body, mesh=mesh, in_specs=in_specs, out_specs=out_specs, check_vma=False)
```

profile of v0, /device:TPU:495, one launch (start us, length us, event | category | flops | bytes accessed | tf_op | source)
XLA Modules:
  0.0 215.9 jit_solution(13414071494126675889)
XLA Ops:
  5.3 1.9 collective-permute-start.2
  7.2 7.5 %collective-permute-start.4 = (f32[256,512]{1,0:T(8,128)}, f32[256,512]{1,0:T(8,128)}, u32[]{:S(2)}, u32[]{:S(2)}) collective-permute-start(f32[256,512]{1,0:T(8,128)} %constant_dynamic-update-slice_fusion), channel_id=1, source_target_pairs={{384,0},{416,32},{448,64},{480,96},{0,128},{32,160},{64,192},{96,2... | collective-permute-start | bytes 1572872 | tf_op jit(solution)/shard_map/ppermute | solution.py:15
  14.7 3.8 %collective-permute-start.6 = (f32[256,512]{1,0:T(8,128)}, f32[256,512]{1,0:T(8,128)}, u32[]{:S(2)}, u32[]{:S(2)}) collective-permute-start(f32[256,512]{1,0:T(8,128)} %constant_dynamic-update-slice_fusion), channel_id=1, source_target_pairs={{256,0},{288,32},{320,64},{352,96},{384,128},{416,160},{448,192},{... | collective-permute-start | bytes 1572872 | tf_op jit(solution)/shard_map/ppermute | solution.py:15
  18.4 4.3 %collective-permute-start.8 = (f32[256,512]{1,0:T(8,128)}, f32[256,512]{1,0:T(8,128)}, u32[]{:S(2)}, u32[]{:S(2)}) collective-permute-start(f32[256,512]{1,0:T(8,128)} %constant_dynamic-update-slice_fusion), channel_id=1, source_target_pairs={{0,1},{1,2},{2,3},{3,4},{4,5},{5,6},{6,7},{7,8},{8,9},{9,10},{10,1... | collective-permute-start | bytes 1572872 | tf_op jit(solution)/shard_map/ppermute | solution.py:21
  32.9 2.4 %fusion.22 = (f32[128,768]{1,0:T(8,128)}, f32[128,768]{1,0:T(8,128)}, f32[128,768]{1,0:T(8,128)}, f32[128,768]{1,0:T(8,128)S(1)}) fusion(f32[256,1536]{1,0:T(8,128)} %param.5), kind=kLoop, calls=%fused_computation.82 | loop fusion | bytes 3145728 | tf_op jit(solution)/shard_map/slice | solution.py:84
  35.3 33.1 %collective-permute-done.2 = f32[256,512]{1,0:T(8,128)} collective-permute-done((f32[256,512]{1,0:T(8,128)}, f32[256,512]{1,0:T(8,128)}, u32[]{:S(2)}, u32[]{:S(2)}) %collective-permute-start.2) | collective-permute-done | bytes 524320 | tf_op jit(solution)/shard_map/ppermute | solution.py:15
  70.4 2.0 copy.74
  74.3 1.9 copy.76
  77.1 2.1 fusion.21
  79.3 5.0 %collective-permute-start.9 = (f32[256,512]{1,0:T(8,128)}, f32[256,512]{1,0:T(8,128)S(1)}, u32[]{:S(2)}, u32[]{:S(2)}) collective-permute-start(f32[256,512]{1,0:T(8,128)} %constant_dynamic-update-slice_fusion), channel_id=1, source_target_pairs={{0,2},{1,3},{2,4},{3,5},{4,6},{5,7},{6,8},{7,9},{8,10},{9,11},{10,... | collective-permute-start | bytes 1572872 | tf_op jit(solution)/shard_map/ppermute | solution.py:21
  85.4 2.3 %collective-permute-start.10 = (f32[256,512]{1,0:T(8,128)}, f32[256,512]{1,0:T(8,128)S(1)}, u32[]{:S(2)}, u32[]{:S(2)}) collective-permute-start(f32[256,512]{1,0:T(8,128)} %constant_dynamic-update-slice_fusion), channel_id=1, source_target_pairs={{0,4},{1,5},{2,6},{3,7},{4,8},{5,9},{6,10},{7,11},{8,12},{9,13},{1... | collective-permute-start | bytes 1572872 | tf_op jit(solution)/shard_map/ppermute | solution.py:21
  87.7 2.5 %collective-permute-start.5 = (f32[256,512]{1,0:T(8,128)}, f32[256,512]{1,0:T(8,128)S(1)}, u32[]{:S(2)}, u32[]{:S(2)}) collective-permute-start(f32[256,512]{1,0:T(8,128)} %collective-permute-done.4), channel_id=1, source_target_pairs={{0,1},{1,2},{2,3},{3,4},{4,5},{5,6},{6,7},{7,8},{8,9},{9,10},{10,1... | collective-permute-start | bytes 1572872 | tf_op jit(solution)/shard_map/ppermute | solution.py:21
  94.8 26.5 %collective-permute-done.5 = f32[256,512]{1,0:T(8,128)S(1)} collective-permute-done((f32[256,512]{1,0:T(8,128)}, f32[256,512]{1,0:T(8,128)S(1)}, u32[]{:S(2)}, u32[]{:S(2)}) %collective-permute-start.5) | collective-permute-done | bytes 524320 | tf_op jit(solution)/shard_map/ppermute | solution.py:21
  124.3 4.4 %collective-permute-done.7 = f32[256,512]{1,0:T(8,128)S(1)} collective-permute-done((f32[256,512]{1,0:T(8,128)}, f32[256,512]{1,0:T(8,128)S(1)}, u32[]{:S(2)}, u32[]{:S(2)}) %collective-permute-start.7) | collective-permute-done | bytes 524320 | tf_op jit(solution)/shard_map/ppermute | solution.py:21
  137.1 26.6 %collective-permute-done.11 = f32[256,512]{1,0:T(8,128)S(1)} collective-permute-done((f32[256,512]{1,0:T(8,128)}, f32[256,512]{1,0:T(8,128)S(1)}, u32[]{:S(2)}, u32[]{:S(2)}) %collective-permute-start.11) | collective-permute-done | bytes 524320 | tf_op jit(solution)/shard_map/ppermute | solution.py:21
  165.2 4.4 %fusion.26 = (f32[6,128]{1,0:T(8,128)S(1)}, f32[6,128,1536]{1,2,0:T(8,128)S(1)}) fusion(f32[128,6,128]{0,2,1:T(8,128)S(1)} %bitcast.95, f32[1536,512]{1,0:T(8,128)S(1)} %get-tuple-element.9, pred[128,1536]{0,1:T(8,128)(4,1)S(1)} %get-tuple-element.29), kind=kOutput, calls=%fused_computation.86 | convolution fusion | flops 1815477504 | bytes 6097920 | tf_op jit(solution)/shard_map/rgd,kd->grk/dot_general | solution.py:102
  170.2 4.0 %fusion.16 = f32[128,6,128]{0,2,1:T(8,128)} fusion(f32[6,128,1536]{1,2,0:T(8,128)S(1)} %get-tuple-element.44, f32[6,128]{1,0:T(8,128)S(1)} %get-tuple-element.43, f32[1536,512]{1,0:T(8,128)S(1)} %get-tuple-element.9, f32[128,6]{0,1:T(8,128)S(1)} %bitcast.98), kind=kOutput, calls=%fused_computation.25 | convolution fusion | flops 1813217280 | bytes 5906432 | tf_op jit(solution)/shard_map/grk,kd->rgd/dot_general | solution.py:111
  176.2 5.6 %fusion.25 = (f32[6,128]{1,0:T(8,128)S(1)}, f32[6,128,1536]{1,2,0:T(8,128)S(1)}) fusion(f32[128,6,128]{0,2,1:T(8,128)} %bitcast.94, f32[1536,512]{1,0:T(8,128)S(1)} %get-tuple-element.9, pred[128,1536]{0,1:T(8,128)(4,1)S(1)} %get-tuple-element.29), kind=kOutput, calls=%fused_computation.85 | convolution fusion | flops 1815477504 | bytes 6097920 | tf_op jit(solution)/shard_map/rgd,kd->grk/dot_general | solution.py:102
  182.3 4.0 %fusion.17 = f32[128,6,128]{0,2,1:T(8,128)} fusion(f32[6,128,1536]{1,2,0:T(8,128)S(1)} %get-tuple-element.42, f32[6,128]{1,0:T(8,128)S(1)} %get-tuple-element.41, f32[1536,512]{1,0:T(8,128)S(1)} %get-tuple-element.9, f32[128,6]{0,1:T(8,128)S(1)} %bitcast.96), kind=kOutput, calls=%fused_computation.26 | convolution fusion | flops 1813217280 | bytes 5906432 | tf_op jit(solution)/shard_map/grk,kd->rgd/dot_general | solution.py:111
  188.3 5.6 %fusion.24 = (f32[6,128]{1,0:T(8,128)S(1)}, f32[6,128,1536]{1,2,0:T(8,128)S(1)}) fusion(f32[128,6,128]{0,2,1:T(8,128)} %bitcast.93, f32[1536,512]{1,0:T(8,128)} %get-tuple-element.10, pred[128,1536]{0,1:T(8,128)(4,1)S(1)} %get-tuple-element.30), kind=kOutput, calls=%fused_computation.84 | convolution fusion | flops 1815477504 | bytes 6097920 | tf_op jit(solution)/shard_map/rgd,kd->grk/dot_general | solution.py:102
  195.8 4.2 %fusion.18 = f32[128,6,128]{0,2,1:T(8,128)} fusion(f32[6,128,1536]{1,2,0:T(8,128)S(1)} %get-tuple-element.40, f32[6,128]{1,0:T(8,128)S(1)} %get-tuple-element.39, f32[1536,512]{1,0:T(8,128)S(1)} %copy-done, f32[128,6]{0,1:T(8,128)S(1)} %bitcast.99), kind=kOutput, calls=%fused_computation.27 | convolution fusion | flops 1813217280 | bytes 5906432 | tf_op jit(solution)/shard_map/grk,kd->rgd/dot_general | solution.py:111
  202.0 5.4 %fusion.23 = (f32[6,128]{1,0:T(8,128)S(1)}, f32[6,128,1536]{1,2,0:T(8,128)S(1)}) fusion(f32[128,6,128]{0,2,1:T(8,128)} %bitcast.92, f32[1536,512]{1,0:T(8,128)S(1)} %copy-done, pred[128,1536]{0,1:T(8,128)(4,1)S(1)} %get-tuple-element.30), kind=kOutput, calls=%fused_computation.83 | convolution fusion | flops 1815477504 | bytes 6097920 | tf_op jit(solution)/shard_map/rgd,kd->grk/dot_general | solution.py:102
  208.0 4.0 %fusion.19 = f32[128,6,128]{0,2,1:T(8,128)} fusion(f32[6,128,1536]{1,2,0:T(8,128)S(1)} %get-tuple-element.38, f32[6,128]{1,0:T(8,128)S(1)} %get-tuple-element.37, f32[1536,512]{1,0:T(8,128)S(1)} %copy-done, f32[128,6]{0,1:T(8,128)S(1)} %bitcast.97), kind=kOutput, calls=%fused_computation.28 | convolution fusion | flops 1813217280 | bytes 5906432 | tf_op jit(solution)/shard_map/grk,kd->rgd/dot_general | solution.py:111
  213.2 2.4 %maximum_maximum_fusion = f32[256,1536]{1,0:T(8,128)} fusion(f32[128,768]{1,0:T(8,128)S(1)} %copy.57, f32[128,768]{1,0:T(8,128)} %copy.56, f32[128,768]{1,0:T(8,128)} %copy.47, f32[128,768]{1,0:T(8,128)S(1)} %copy-done.1), kind=kLoop, calls=%fused_computation.20 | loop fusion | flops 1179648 | bytes 3145728 | tf_op jit(solution)/shard_map/concatenate | solution.py:120
  (59 shorter events, 49.4 us)
Async XLA Ops:
  3.3 26.3 %collective-permute-start = (f32[256,512]{1,0:T(8,128)}, f32[256,512]{1,0:T(8,128)}, u32[]{:S(2)}, u32[]{:S(2)}) collective-permute-start(f32[256,512]{1,0:T(8,128)} %constant_dynamic-update-slice_fusion), channel_id=1, source_target_pairs={{480,0},{0,32},{32,64},{64,96},{96,128},{128,160},{160,192},{192,2... | collective-permute-start | bytes 1572872 | tf_op jit(solution)/shard_map/ppermute | solution.py:15
  5.3 63.2 %collective-permute-start.2 = (f32[256,512]{1,0:T(8,128)}, f32[256,512]{1,0:T(8,128)}, u32[]{:S(2)}, u32[]{:S(2)}) collective-permute-start(f32[256,512]{1,0:T(8,128)} %constant_dynamic-update-slice_fusion), channel_id=1, source_target_pairs={{448,0},{480,32},{0,64},{32,96},{64,128},{96,160},{128,192},{160,2... | collective-permute-start | bytes 1572872 | tf_op jit(solution)/shard_map/ppermute | solution.py:15
  7.2 78.2 %collective-permute-start.4 = (f32[256,512]{1,0:T(8,128)}, f32[256,512]{1,0:T(8,128)}, u32[]{:S(2)}, u32[]{:S(2)}) collective-permute-start(f32[256,512]{1,0:T(8,128)} %constant_dynamic-update-slice_fusion), channel_id=1, source_target_pairs={{384,0},{416,32},{448,64},{480,96},{0,128},{32,160},{64,192},{96,2... | collective-permute-start | bytes 1572872 | tf_op jit(solution)/shard_map/ppermute | solution.py:15
  14.7 73.0 %collective-permute-start.6 = (f32[256,512]{1,0:T(8,128)}, f32[256,512]{1,0:T(8,128)}, u32[]{:S(2)}, u32[]{:S(2)}) collective-permute-start(f32[256,512]{1,0:T(8,128)} %constant_dynamic-update-slice_fusion), channel_id=1, source_target_pairs={{256,0},{288,32},{320,64},{352,96},{384,128},{416,160},{448,192},{... | collective-permute-start | bytes 1572872 | tf_op jit(solution)/shard_map/ppermute | solution.py:15
  18.4 115.4 %collective-permute-start.8 = (f32[256,512]{1,0:T(8,128)}, f32[256,512]{1,0:T(8,128)}, u32[]{:S(2)}, u32[]{:S(2)}) collective-permute-start(f32[256,512]{1,0:T(8,128)} %constant_dynamic-update-slice_fusion), channel_id=1, source_target_pairs={{0,1},{1,2},{2,3},{3,4},{4,5},{5,6},{6,7},{7,8},{8,9},{9,10},{10,1... | collective-permute-start | bytes 1572872 | tf_op jit(solution)/shard_map/ppermute | solution.py:21
  29.7 49.6 %collective-permute-start.1 = (f32[256,512]{1,0:T(8,128)}, f32[256,512]{1,0:T(8,128)}, u32[]{:S(2)}, u32[]{:S(2)}) collective-permute-start(f32[256,512]{1,0:T(8,128)} %collective-permute-done), channel_id=1, source_target_pairs={{0,1},{1,2},{2,3},{3,4},{4,5},{5,6},{6,7},{7,8},{8,9},{9,10},{10,1... | collective-permute-start | bytes 1572872 | tf_op jit(solution)/shard_map/ppermute | solution.py:21
  68.4 21.8 %collective-permute-start.3 = (f32[256,512]{1,0:T(8,128)}, f32[256,512]{1,0:T(8,128)}, u32[]{:S(2)}, u32[]{:S(2)}) collective-permute-start(f32[256,512]{1,0:T(8,128)} %collective-permute-done.2), channel_id=1, source_target_pairs={{0,1},{1,2},{2,3},{3,4},{4,5},{5,6},{6,7},{7,8},{8,9},{9,10},{10,1... | collective-permute-start | bytes 1572872 | tf_op jit(solution)/shard_map/ppermute | solution.py:21
  79.3 56.3 %collective-permute-start.9 = (f32[256,512]{1,0:T(8,128)}, f32[256,512]{1,0:T(8,128)S(1)}, u32[]{:S(2)}, u32[]{:S(2)}) collective-permute-start(f32[256,512]{1,0:T(8,128)} %constant_dynamic-update-slice_fusion), channel_id=1, source_target_pairs={{0,2},{1,3},{2,4},{3,5},{4,6},{5,7},{6,8},{7,9},{8,10},{9,11},{10,... | collective-permute-start | bytes 1572872 | tf_op jit(solution)/shard_map/ppermute | solution.py:21
  85.4 50.9 %collective-permute-start.10 = (f32[256,512]{1,0:T(8,128)}, f32[256,512]{1,0:T(8,128)S(1)}, u32[]{:S(2)}, u32[]{:S(2)}) collective-permute-start(f32[256,512]{1,0:T(8,128)} %constant_dynamic-update-slice_fusion), channel_id=1, source_target_pairs={{0,4},{1,5},{2,6},{3,7},{4,8},{5,9},{6,10},{7,11},{8,12},{9,13},{1... | collective-permute-start | bytes 1572872 | tf_op jit(solution)/shard_map/ppermute | solution.py:21
  87.7 33.5 %collective-permute-start.5 = (f32[256,512]{1,0:T(8,128)}, f32[256,512]{1,0:T(8,128)S(1)}, u32[]{:S(2)}, u32[]{:S(2)}) collective-permute-start(f32[256,512]{1,0:T(8,128)} %collective-permute-done.4), channel_id=1, source_target_pairs={{0,1},{1,2},{2,3},{3,4},{4,5},{5,6},{6,7},{7,8},{8,9},{9,10},{10,1... | collective-permute-start | bytes 1572872 | tf_op jit(solution)/shard_map/ppermute | solution.py:21
  90.2 38.5 %collective-permute-start.7 = (f32[256,512]{1,0:T(8,128)}, f32[256,512]{1,0:T(8,128)S(1)}, u32[]{:S(2)}, u32[]{:S(2)}) collective-permute-start(f32[256,512]{1,0:T(8,128)} %collective-permute-done.6), channel_id=1, source_target_pairs={{0,1},{1,2},{2,3},{3,4},{4,5},{5,6},{6,7},{7,8},{8,9},{9,10},{10,1... | collective-permute-start | bytes 1572872 | tf_op jit(solution)/shard_map/ppermute | solution.py:21
  121.3 42.4 %collective-permute-start.11 = (f32[256,512]{1,0:T(8,128)}, f32[256,512]{1,0:T(8,128)S(1)}, u32[]{:S(2)}, u32[]{:S(2)}) collective-permute-start(f32[256,512]{1,0:T(8,128)} %constant_dynamic-update-slice_fusion), channel_id=1, source_target_pairs={{0,8},{1,9},{2,10},{3,11},{4,12},{5,13},{6,14},{7,15},{8,16},{9,17... | collective-permute-start | bytes 1572872 | tf_op jit(solution)/shard_map/ppermute | solution.py:21
  128.7 35.7 %collective-permute-start.12 = (f32[256,512]{1,0:T(8,128)}, f32[256,512]{1,0:T(8,128)S(1)}, u32[]{:S(2)}, u32[]{:S(2)}) collective-permute-start(f32[256,512]{1,0:T(8,128)} %constant_dynamic-update-slice_fusion), channel_id=1, source_target_pairs={{0,16},{1,17},{2,18},{3,19},{4,20},{5,21},{6,22},{7,23},{8,24},{9,... | collective-permute-start | bytes 1572872 | tf_op jit(solution)/shard_map/ppermute | solution.py:21
  133.1 32.1 %copy-start.2 = (f32[128,768]{0,1:T(8,128)S(1)}, f32[128,768]{0,1:T(8,128)}, u32[]{:S(2)}) copy-start(f32[128,768]{0,1:T(8,128)} %copy.74) | copy-start | bytes 1179652
  193.9 1.9 copy-start
  208.0 5.2 %copy-start.1 = (f32[128,768]{1,0:T(8,128)S(1)}, f32[128,768]{1,0:T(8,128)}, u32[]{:S(2)}) copy-start(f32[128,768]{1,0:T(8,128)} %copy.46) | copy-start | bytes 1179652
where the time goes:
time: 220 us; the launch traced here: 216 us
  waiting for transfers between devices  90.7 us (41%)
  starting transfers between devices  38.5 us (18%)
  matrix products  37.2 us (17%)
  local copies, waits for them, and re-layouts  35.8 us (16%)
  other arithmetic  13.1 us (6%)
    ppermute x9, waiting for transfers between devices, shifted_2(): return lax.ppermute(block, axis, route)  57.5 us
    ppermute x4, waiting for transfers between devices, shifted(): return lax.ppermute(block, axis, route)  33.2 us
    ppermute x9, starting transfers between devices, shifted_2(): return lax.ppermute(block, axis, route)  23.4 us
    dot_general x4, matrix products, body(): jnp.einsum('rgd,kd->grk', query_portion, key_portion, precision=lax.Preci...  20.9 us
    unnamed x24, local copies, waits for them, and re-layouts  20.7 us
    dot_general x4, matrix products, body(): jnp.einsum('grk,kd->rgd', weights, value_portion, precision=lax.Precision...  16.3 us
    ppermute x4, starting transfers between devices, shifted(): return lax.ppermute(block, axis, route)  15.1 us
    reshape x4, local copies, waits for them, and re-layouts, body(): (weighted / jnp.transpose(denominator)[:, :, None]).reshape(BLOCK_TOKENS,...  6.88 us
  transfers between devices with their start and end apart: 13, of which 4 were waited for; matrix products, arithmetic and copies ran while one was open for 15% of the time, Pallas kernels for 0%

commit v1 on v0

v1 whole, which is shorter than its diff:
```python
import jax
import jax.numpy as jnp
from jax import lax
from jax.experimental import pallas as pl
from jax.experimental.pallas import tpu as pltpu
from jax.sharding import PartitionSpec as P

HEADS, GROUPS, FEATURES, BLOCK = 12, 2, 128, 128
PER_GROUP = HEADS // GROUPS
SLOTS = 15
ROWS, COLS = 256, 512
OFFSETS = (1, 2, 4, 8, 16, 32, 64, 128, 256)
OWN = 0
SLOT = {o: i + 1 for i, o in enumerate(OFFSETS)}
RELAY_Z, RELAY_Y = 10, 11
BUFFERS = 12
RULES = ("1", "2", "2b", "4", "4f", "4a", "8", "16", "32", "64", "128", "256", "256a")
CHUNKS = 8
CHUNK = ROWS // CHUNKS
STAGES = (("64", 0), ("8", 0), ("1", 1), ("y", 3), ("128", 2), ("2", 3), ("z", 5))
NEG = -1e30
MESH = pl.DeviceIdType.MESH

STEPS = (
    (((0, 0), (8, 0)), ((1, 0), (1, 1)), ((16, 0), (32, 0)), ((64, 0), (128, 0)), ((2, 0), (2, 1)), ((4, 0), (256, 0))),
    (((0, 0), (0, 1)), ((1, 0), (1, 1)), ((8, 1), (16, 1)), ((32, 1), (64, 1)), ((2, 1), (128, 1)), ((4, 1), (256, 1))),
)


def pick(index, values):
    out = jnp.int32(values[0])
    for i, v in enumerate(values[1:], 1):
        if v != values[i - 1]:
            out = jnp.where(index >= i, jnp.int32(v), out)
    return out


def split(a):
    hi = a.astype(jnp.bfloat16)
    return hi, (a - hi.astype(jnp.float32)).astype(jnp.bfloat16)


def kernel(q_ref, k_ref, v_ref, lists_ref, out_ref, buf, q_vmem, q_cat, acc, top, total, ssem, rsem, lsem):
    lo, hi = lax.axis_index("ctxlo"), lax.axis_index("ctxhi")
    h, z = lo // 8, lo % 8
    y, g, c = hi // 4, (hi // 2) % 2, hi % 2
    x = h * 2 + g
    shard = hi * 16 + lo

    def dev(dy, dx, dz, core):
        xx = (x + dx + 4) % 4
        return {"ctxlo": (xx // 2) * 8 + (z + dz + 8) % 8, "ctxhi": ((y + dy + 8) % 8) * 4 + (xx % 2) * 2 + core}

    k_copy = pltpu.make_async_copy(k_ref, buf.at[OWN, :, pl.ds(0, 256)], lsem.at[0])
    v_copy = pltpu.make_async_copy(v_ref, buf.at[OWN, :, pl.ds(256, 256)], lsem.at[1])
    q_copy = pltpu.make_async_copy(q_ref, q_vmem, lsem.at[2])
    k_copy.start()
    v_copy.start()
    q_copy.start()
    barrier = pltpu.get_barrier_semaphore()
    f = 1 - c
    peers = [dev(0, 0, 1, c), dev(0, 0, -1, c), dev(0, 0, 2, c), dev(0, 0, -2, c), dev(1, 0, 0, c), dev(-1, 0, 0, c),
             dev(2, 0, 0, c), dev(-2, 0, 0, c), dev(0, 1, 0, c), dev(0, -1, 0, c), dev(0, 1, 0, f), dev(0, -1, 0, f),
             dev(0, 2, 0, c), dev(0, 2, 0, f), dev(0, 0, 0, f)]
    for peer in peers:
        pl.semaphore_signal(barrier, 1, device_id=peer, device_id_type=MESH)
    k_copy.wait()
    v_copy.wait()
    pl.semaphore_wait(barrier, len(peers))

    def rows(k):
        return pl.ds(pl.multiple_of(k * CHUNK, CHUNK), CHUNK)

    def send(rule, src, dst, k, target):
        return pltpu.make_async_remote_copy(
            src_ref=buf.at[src, rows(k)], dst_ref=buf.at[dst, rows(k)],
            send_sem=ssem.at[RULES.index(rule), k], recv_sem=rsem.at[dst, k],
            device_id=target, device_id_type=MESH)

    def arrive(dst, k):
        send("1", dst, dst, k, peers[0]).wait_recv()

    t1, tz2, tzm2 = peers[0], peers[2], peers[3]
    y1, y2, ym2 = peers[4], peers[6], peers[7]
    side = jnp.where(g == 0, 1, -1)
    t32 = dev(0, side, 0, c)
    t16 = dev(0, jnp.where(c == 0, 0, side), 0, f)
    top_x = h == 1
    carry = top_x & (c == 1)
    t8 = dev(0, jnp.where(carry, -side, 2), 0, jnp.where(top_x, f, c))
    g1 = g == 1
    y16 = g1 & (c == 1)
    y8 = g1 & carry
    z_minus = (z == 1) | (z == 3) | (z == 4) | (z == 5) | (z == 7)
    z_forward = (z == 7) | (z == 1) | (z == 2) | (z == 3) | (z == 5)
    z_plus = (z == 0) | (z == 2) | (z == 4)
    z_high = z >= 4
    y_odd = y % 2 == 1
    no = jnp.logical_not

    def when(condition, action):
        pl.when(condition)(action)

    def first(k, _):
        send("64", OWN, SLOT[64], k, y1).start()
        when(no(y8), lambda: send("8", OWN, SLOT[8], k, t8).start())
        when(z < 7, lambda: send("1", OWN, SLOT[1], k, t1).start())
        when(no(g1), lambda: send("32", OWN, SLOT[32], k, t32).start())
        when(no(y16), lambda: send("16", OWN, SLOT[16], k, t16).start())
        when(z_minus & no(z_high), lambda: send("4a", OWN, RELAY_Z, k, tzm2).start())
        when(y_odd, lambda: send("256a", OWN, RELAY_Y, k, ym2).start())
        return 0

    lax.fori_loop(0, CHUNKS, first, 0)

    def s64(k):
        arrive(SLOT[64], k)
        send("128", SLOT[64], SLOT[128], k, y1).start()
        when(y8, lambda: send("8", SLOT[64], SLOT[8], k, t8).start())
        when(g1, lambda: send("32", SLOT[64], SLOT[32], k, t32).start())
        when(y16, lambda: send("16", SLOT[64], SLOT[16], k, t16).start())

    def s8(k):
        arrive(SLOT[8], k)
        when(z == 7, lambda: send("1", SLOT[8], SLOT[1], k, t1).start())
        when(z == 6, lambda: send("2b", SLOT[8], SLOT[2], k, tz2).start())
        when(z_minus & z_high, lambda: send("4a", SLOT[8], RELAY_Z, k, tzm2).start())

    def s1(k):
        arrive(SLOT[1], k)
        when(z < 7, lambda: send("2", SLOT[1], SLOT[2], k, t1).start())

    def s2(k):
        arrive(SLOT[2], k)
        when(z_plus, lambda: send("4", SLOT[2], SLOT[4], k, tz2).start())

    def sz(k):
        @pl.when(z_forward)
        def _():
            arrive(RELAY_Z, k)
            send("4f", RELAY_Z, SLOT[4], k, tzm2).start()

    def s128(k):
        arrive(SLOT[128], k)
        when(no(y_odd), lambda: send("256", SLOT[128], SLOT[256], k, y2).start())

    def sy(k):
        @pl.when(y_odd)
        def _():
            arrive(RELAY_Y, k)
            send("256", RELAY_Y, SLOT[256], k, ym2).start()

    stage = {"64": s64, "8": s8, "1": s1, "2": s2, "z": sz, "128": s128, "y": sy}
    depth = max(d for _, d in STAGES)

    q_copy.wait()
    scale = jnp.float32(FEATURES ** -0.5 * 1.4426950408889634)
    for b in range(2):
        for n in range(HEADS):
            part = q_vmem[b * BLOCK:(b + 1) * BLOCK, n * FEATURES:(n + 1) * FEATURES] * scale
            high, low = split(part)
            at = pl.ds((n % PER_GROUP) * BLOCK, BLOCK)
            q_cat[b, n // PER_GROUP, at, 0:FEATURES] = high
            q_cat[b, n // PER_GROUP, at, FEATURES:] = low
    acc[...] = jnp.zeros_like(acc)
    total[...] = jnp.zeros_like(total)
    top[...] = jnp.full_like(top, NEG)

    def relay(t, _):
        for name, d in STAGES:
            when((t >= d) & (t < CHUNKS + d), lambda name=name, d=d: stage[name](t - d))
        return 0

    lax.fori_loop(0, CHUNKS + depth, relay, 0)

    col = lax.broadcasted_iota(jnp.int32, (BLOCK, 256), 1)
    row = lax.broadcasted_iota(jnp.int32, (BLOCK, 256), 0)

    def wait_all(offsets):
        def body(k, _):
            for o in offsets:
                arrive(SLOT[o], k)
            return 0
        lax.fori_loop(0, CHUNKS, body, 0)

    def step(i, _):
        j, b = i // 2, i % 2
        when(i == 4, lambda: wait_all((16, 32)))
        when(i == 10, lambda: wait_all((4, 256)))
        where = []
        distance = []
        for p in range(2):
            o = pick(i, [STEPS[n % 2][n // 2][p][0] for n in range(12)])
            s = pick(i, [SLOT.get(STEPS[n % 2][n // 2][p][0], OWN) for n in range(12)])
            kb = pick(i, [STEPS[n % 2][n // 2][p][1] for n in range(12)])
            where.append((s, pl.ds(pl.multiple_of(kb * BLOCK, BLOCK), BLOCK)))
            distance.append(2 * o + b - kb)
        away = jnp.where(col < BLOCK, distance[0], distance[1])
        target = shard * 2 + b - away
        hit = target[0:8] == lists_ref[b, 0]
        for n in range(1, SLOTS):
            hit = hit | (target[0:8] == lists_ref[b, n])
        bias8 = jnp.where(hit & (target[0:8] >= 0), jnp.float32(0), jnp.float32(NEG))
        bias = jnp.where((away > 0) | (col % BLOCK <= row), jnp.broadcast_to(bias8[0:1], (BLOCK, 256)), jnp.float32(NEG))
        for n in range(GROUPS):
            keys = jnp.concatenate([buf[s, r, n * FEATURES:(n + 1) * FEATURES] for s, r in where], axis=0)
            values = jnp.concatenate([buf[s, r, 256 + n * FEATURES:256 + (n + 1) * FEATURES] for s, r in where], axis=0)
            k_high, k_low = split(keys)
            v_high, v_low = split(values)
            k_high = jnp.concatenate([k_high, k_high], axis=1)
            k_low = jnp.concatenate([k_low, k_low], axis=1)
            v_both = jnp.concatenate([v_high, v_low], axis=1)
            q = q_cat[b, n]
            dims = (((1,), (1,)), ((), ()))
            scores = lax.dot_general(q, k_high, dims, preferred_element_type=jnp.float32)
            scores = scores + lax.dot_general(q, k_low, dims, preferred_element_type=jnp.float32)
            scores = (scores.reshape(PER_GROUP, BLOCK, 256) + bias[None]).reshape(PER_GROUP * BLOCK, 256)
            old = top[b, n]
            new = jnp.maximum(old, jnp.max(scores, axis=1, keepdims=True))
            weights = jnp.exp2(scores - jnp.concatenate([new, new], axis=1))
            alpha = jnp.exp2(old - new)
            top[b, n] = new
            total[b, n] = total[b, n] * alpha + weights[:, :128] + weights[:, 128:]
            w_high, w_low = split(weights)
            o = jnp.dot(w_high, v_both, preferred_element_type=jnp.float32)
            o = o + jnp.dot(w_low, v_both, preferred_element_type=jnp.float32)
            acc[b, n] = acc[b, n] * alpha + o[:, :128] + o[:, 128:]
        return 0

    lax.fori_loop(0, 12, step, 0)

    for b in range(2):
        for n in range(GROUPS):
            out = acc[b, n] / jnp.sum(total[b, n], axis=1, keepdims=True)
            for r in range(PER_GROUP):
                m = n * PER_GROUP + r
                out_ref[b * BLOCK:(b + 1) * BLOCK, m * FEATURES:(m + 1) * FEATURES] = out[r * BLOCK:(r + 1) * BLOCK]

    def finish(k, _):
        def sent(rule):
            send(rule, OWN, SLOT[64], k, t1).wait_send()
        for rule in ("64", "8", "1", "32", "16", "128", "256"):
            sent(rule)
        when(z < 7, lambda: sent("2"))
        when(z == 6, lambda: sent("2b"))
        when(z_plus, lambda: sent("4"))
        when(z_forward, lambda: sent("4f"))
        when(z_minus, lambda: sent("4a"))
        when(y_odd, lambda: sent("256a"))
        return 0

    lax.fori_loop(0, CHUNKS, finish, 0)


def body(query_matrix, key_matrix, value_matrix, block_lists):
    pair = (2, GROUPS, PER_GROUP * BLOCK)
    return pl.pallas_call(
        kernel,
        out_shape=jax.ShapeDtypeStruct((ROWS, HEADS * FEATURES), jnp.float32),
        in_specs=[pl.BlockSpec(memory_space=pl.ANY)] * 3 + [pl.BlockSpec(memory_space=pltpu.SMEM)],
        out_specs=pl.BlockSpec(memory_space=pltpu.VMEM),
        scratch_shapes=[
            pltpu.VMEM((BUFFERS, ROWS, COLS), jnp.float32),
            pltpu.VMEM((ROWS, HEADS * FEATURES), jnp.float32),
            pltpu.VMEM(pair + (256,), jnp.bfloat16),
            pltpu.VMEM(pair + (FEATURES,), jnp.float32),
            pltpu.VMEM(pair + (128,), jnp.float32),
            pltpu.VMEM(pair + (128,), jnp.float32),
            pltpu.SemaphoreType.DMA((len(RULES), CHUNKS)),
            pltpu.SemaphoreType.DMA((BUFFERS, CHUNKS)),
            pltpu.SemaphoreType.DMA((3,)),
        ],
        compiler_params=pltpu.CompilerParams(collective_id=0, has_side_effects=True, vmem_limit_bytes=56 << 20),
    )(query_matrix, key_matrix, value_matrix, block_lists)


def solution(mesh):
    spec = P(("ctxhi", "ctxlo"), None)
    return jax.shard_map(body, mesh=mesh, in_specs=(spec,) * 4, out_specs=spec, check_vma=False)
```

time: 220 us -> 82.5 us (0.38)
  the two profiles are of different devices: /device:TPU:495 before, /device:TPU:128 now
where the time goes in v1:
time: 82.5 us; the launch traced here: 82.3 us
  Pallas kernels  79.7 us (97%)
  local copies, waits for them, and re-layouts  2.66 us (3%)
    pallas_call x1, Pallas kernels, body(): pl.pallas_call(kernel, out_shape=jax.ShapeDtypeStruct((ROWS, HEADS * FEAT...  79.7 us
    unnamed x1, local copies, waits for them, and re-layouts  2.66 us

profile of v1, /device:TPU:128, one launch (start us, length us, event | category | flops | bytes accessed | tf_op | source)
XLA Modules:
  0.0 82.3 jit_solution(7606699521012134866)
XLA Ops:
  0.0 79.7 %shard_map.46 = f32[256,1536]{1,0:T(8,128)} custom-call(f32[256,1536]{1,0:T(8,128)} %q_ref.1, f32[256,256]{1,0:T(8,128)} %k_ref.1, f32[256,256]{1,0:T(8,128)} %v_ref.1, s32[2,15]{1,0:T(2,128)} %lists_ref.1), custom_call_target="tpu_custom_call" | custom-call | tf_op jit(solution)/shard_map/pallas_call | solution.py:257
  79.7 2.7 %copy.6 = f32[256,1536]{1,0:T(8,128)} copy(f32[256,1536]{1,0:T(8,128)} %shard_map.46) | data formatting | bytes 3145728

commit v2 on v1

--- a/solution.py
+++ b/solution.py
@@ -17,13 +17,17 @@
 RULES = ("1", "2", "2b", "4", "4f", "4a", "8", "16", "32", "64", "128", "256", "256a")
 CHUNKS = 8
 CHUNK = ROWS // CHUNKS
-STAGES = (("64", 0), ("8", 0), ("1", 1), ("y", 3), ("128", 2), ("2", 3), ("z", 5))
+Z_BACK = (2, 6, 1, 6, 8, 8, 1, 6)
+Y_BACK = 4
+STAGES = (("8", 0), ("64", 0), ("1", 0), ("own 32", 4), ("32", 8), ("z", 8), ("y", 8), ("2", 8), ("128", 8))
+TURNS = 28
+WORK = {1: 0, 2: 1, 4: 2, 5: 3, **{t: t - 4 for t in range(8, TURNS)}}
 NEG = -1e30
 MESH = pl.DeviceIdType.MESH
 
 STEPS = (
-    (((0, 0), (8, 0)), ((1, 0), (1, 1)), ((16, 0), (32, 0)), ((64, 0), (128, 0)), ((2, 0), (2, 1)), ((4, 0), (256, 0))),
-    (((0, 0), (0, 1)), ((1, 0), (1, 1)), ((8, 1), (16, 1)), ((32, 1), (64, 1)), ((2, 1), (128, 1)), ((4, 1), (256, 1))),
+    (1, (0, 0), (0, 1)), (0, (0, 0), (8, 0)), (0, (1, 0), (1, 1)), (1, (1, 0), (1, 1)), (1, (8, 1), (64, 1)), (0, (64, 0), (128, 0)),
+    (0, (2, 0), (2, 1)), (1, (2, 1), (128, 1)), (0, (32, 0), (16, 0)), (1, (32, 1), (16, 1)), (0, (4, 0), (256, 0)), (1, (4, 1), (256, 1)),
 )
 
 
@@ -81,50 +85,58 @@
         send("1", dst, dst, k, peers[0]).wait_recv()
 
     t1, tz2, tzm2 = peers[0], peers[2], peers[3]
+
+    def z_back(away):
+        return pick(z, [Z_BACK[(i + away) % 8] for i in range(8)])
+
+    back_own, back_relay, back_plus = z_back(0), z_back(2), z_back(-2)
     y1, y2, ym2 = peers[4], peers[6], peers[7]
     side = jnp.where(g == 0, 1, -1)
     t32 = dev(0, side, 0, c)
-    t16 = dev(0, jnp.where(c == 0, 0, side), 0, f)
+    t16 = dev(0, 0, 0, f)
     top_x = h == 1
     carry = top_x & (c == 1)
     t8 = dev(0, jnp.where(carry, -side, 2), 0, jnp.where(top_x, f, c))
     g1 = g == 1
-    y16 = g1 & (c == 1)
     y8 = g1 & carry
-    z_minus = (z == 1) | (z == 3) | (z == 4) | (z == 5) | (z == 7)
-    z_forward = (z == 7) | (z == 1) | (z == 2) | (z == 3) | (z == 5)
-    z_plus = (z == 0) | (z == 2) | (z == 4)
     z_high = z >= 4
-    y_odd = y % 2 == 1
     no = jnp.logical_not
 
     def when(condition, action):
         pl.when(condition)(action)
 
-    def first(k, _):
-        send("64", OWN, SLOT[64], k, y1).start()
-        when(no(y8), lambda: send("8", OWN, SLOT[8], k, t8).start())
-        when(z < 7, lambda: send("1", OWN, SLOT[1], k, t1).start())
-        when(no(g1), lambda: send("32", OWN, SLOT[32], k, t32).start())
-        when(no(y16), lambda: send("16", OWN, SLOT[16], k, t16).start())
-        when(z_minus & no(z_high), lambda: send("4a", OWN, RELAY_Z, k, tzm2).start())
-        when(y_odd, lambda: send("256a", OWN, RELAY_Y, k, ym2).start())
-        return 0
-
-    lax.fori_loop(0, CHUNKS, first, 0)
+    def own(rule, dst, target, condition=None):
+        def go(k):
+            if condition is None:
+                send(rule, OWN, dst, k, target).start()
+            else:
+                when(condition(k), lambda: send(rule, OWN, dst, k, target).start())
+        return go
+
+    own_32 = own("32", SLOT[32], t32, lambda k: no(g1))
+    for go in (own("64", SLOT[64], y1), own("8", SLOT[8], t8, lambda k: no(y8)), own("1", SLOT[1], t1, lambda k: z < 7),
+               own("4a", RELAY_Z, tzm2, lambda k: (k < back_own) & no(z_high)),
+               own("16", SLOT[16], t16, lambda k: c == 0), own("256a", RELAY_Y, ym2, lambda k: k < Y_BACK)):
+        def first(k, _, go=go):
+            go(k)
+            return 0
+        lax.fori_loop(0, CHUNKS, first, 0)
 
     def s64(k):
         arrive(SLOT[64], k)
         send("128", SLOT[64], SLOT[128], k, y1).start()
         when(y8, lambda: send("8", SLOT[64], SLOT[8], k, t8).start())
         when(g1, lambda: send("32", SLOT[64], SLOT[32], k, t32).start())
-        when(y16, lambda: send("16", SLOT[64], SLOT[16], k, t16).start())
+
+    def s32(k):
+        arrive(SLOT[32], k)
+        when(c == 1, lambda: send("16", SLOT[32], SLOT[16], k, t16).start())
 
     def s8(k):
         arrive(SLOT[8], k)
+        when(z == 6, lambda: send("2b", SLOT[8], SLOT[2], k, tz2).start())
         when(z == 7, lambda: send("1", SLOT[8], SLOT[1], k, t1).start())
-        when(z == 6, lambda: send("2b", SLOT[8], SLOT[2], k, tz2).start())
-        when(z_minus & z_high, lambda: send("4a", SLOT[8], RELAY_Z, k, tzm2).start())
+        when((k < back_own) & z_high, lambda: send("4a", SLOT[8], RELAY_Z, k, tzm2).start())
 
     def s1(k):
         arrive(SLOT[1], k)
@@ -132,26 +144,25 @@
 
     def s2(k):
         arrive(SLOT[2], k)
-        when(z_plus, lambda: send("4", SLOT[2], SLOT[4], k, tz2).start())
+        when(k >= back_plus, lambda: send("4", SLOT[2], SLOT[4], k, tz2).start())
 
     def sz(k):
-        @pl.when(z_forward)
+        @pl.when(k < back_relay)
         def _():
             arrive(RELAY_Z, k)
             send("4f", RELAY_Z, SLOT[4], k, tzm2).start()
 
     def s128(k):
         arrive(SLOT[128], k)
-        when(no(y_odd), lambda: send("256", SLOT[128], SLOT[256], k, y2).start())
+        when(k >= Y_BACK, lambda: send("256", SLOT[128], SLOT[256], k, y2).start())
 
     def sy(k):
-        @pl.when(y_odd)
+        @pl.when(k < Y_BACK)
         def _():
             arrive(RELAY_Y, k)
             send("256", RELAY_Y, SLOT[256], k, ym2).start()
 
-    stage = {"64": s64, "8": s8, "1": s1, "2": s2, "z": sz, "128": s128, "y": sy}
-    depth = max(d for _, d in STAGES)
+    stage = {"64": s64, "8": s8, "1": s1, "2": s2, "z": sz, "128": s128, "y": sy, "32": s32, "own 32": own_32}
 
     q_copy.wait()
     scale = jnp.float32(FEATURES ** -0.5 * 1.4426950408889634)
@@ -166,13 +177,6 @@
     total[...] = jnp.zeros_like(total)
     top[...] = jnp.full_like(top, NEG)
 
-    def relay(t, _):
-        for name, d in STAGES:
-            when((t >= d) & (t < CHUNKS + d), lambda name=name, d=d: stage[name](t - d))
-        return 0
-
-    lax.fori_loop(0, CHUNKS + depth, relay, 0)
-
     col = lax.broadcasted_iota(jnp.int32, (BLOCK, 256), 1)
     row = lax.broadcasted_iota(jnp.int32, (BLOCK, 256), 0)
 
@@ -183,51 +187,62 @@
             return 0
         lax.fori_loop(0, CHUNKS, body, 0)
 
-    def step(i, _):
-        j, b = i // 2, i % 2
-        when(i == 4, lambda: wait_all((16, 32)))
-        when(i == 10, lambda: wait_all((4, 256)))
+    def step(i, n):
+        b = pick(i, [s[0] for s in STEPS])
         where = []
         distance = []
-        for p in range(2):
-            o = pick(i, [STEPS[n % 2][n // 2][p][0] for n in range(12)])
-            s = pick(i, [SLOT.get(STEPS[n % 2][n // 2][p][0], OWN) for n in range(12)])
-            kb = pick(i, [STEPS[n % 2][n // 2][p][1] for n in range(12)])
-            where.append((s, pl.ds(pl.multiple_of(kb * BLOCK, BLOCK), BLOCK)))
+        for p in (1, 2):
+            o = pick(i, [s[p][0] for s in STEPS])
+            slot = pick(i, [SLOT.get(s[p][0], OWN) for s in STEPS])
+            kb = pick(i, [s[p][1] for s in STEPS])
+            where.append((slot, pl.ds(pl.multiple_of(kb * BLOCK, BLOCK), BLOCK)))
             distance.append(2 * o + b - kb)
         away = jnp.where(col < BLOCK, distance[0], distance[1])
         target = shard * 2 + b - away
         hit = target[0:8] == lists_ref[b, 0]
-        for n in range(1, SLOTS):
-            hit = hit | (target[0:8] == lists_ref[b, n])
+        for m in range(1, SLOTS):
+            hit = hit | (target[0:8] == lists_ref[b, m])
         bias8 = jnp.where(hit & (target[0:8] >= 0), jnp.float32(0), jnp.float32(NEG))
         bias = jnp.where((away > 0) | (col % BLOCK <= row), jnp.broadcast_to(bias8[0:1], (BLOCK, 256)), jnp.float32(NEG))
-        for n in range(GROUPS):
-            keys = jnp.concatenate([buf[s, r, n * FEATURES:(n + 1) * FEATURES] for s, r in where], axis=0)
-            values = jnp.concatenate([buf[s, r, 256 + n * FEATURES:256 + (n + 1) * FEATURES] for s, r in where], axis=0)
-            k_high, k_low = split(keys)
-            v_high, v_low = split(values)
-            k_high = jnp.concatenate([k_high, k_high], axis=1)
-            k_low = jnp.concatenate([k_low, k_low], axis=1)
-            v_both = jnp.concatenate([v_high, v_low], axis=1)
-            q = q_cat[b, n]
-            dims = (((1,), (1,)), ((), ()))
-            scores = lax.dot_general(q, k_high, dims, preferred_element_type=jnp.float32)
-            scores = scores + lax.dot_general(q, k_low, dims, preferred_element_type=jnp.float32)
-            scores = (scores.reshape(PER_GROUP, BLOCK, 256) + bias[None]).reshape(PER_GROUP * BLOCK, 256)
-            old = top[b, n]
-            new = jnp.maximum(old, jnp.max(scores, axis=1, keepdims=True))
-            weights = jnp.exp2(scores - jnp.concatenate([new, new], axis=1))
-            alpha = jnp.exp2(old - new)
-            top[b, n] = new
-            total[b, n] = total[b, n] * alpha + weights[:, :128] + weights[:, 128:]
-            w_high, w_low = split(weights)
-            o = jnp.dot(w_high, v_both, preferred_element_type=jnp.float32)
-            o = o + jnp.dot(w_low, v_both, preferred_element_type=jnp.float32)
-            acc[b, n] = acc[b, n] * alpha + o[:, :128] + o[:, 128:]
+        def lanes(start):
+            return pl.ds(pl.multiple_of(start + n * FEATURES, FEATURES), FEATURES)
+
+        keys = jnp.concatenate([buf[s, r, lanes(0)] for s, r in where], axis=0)
+        values = jnp.concatenate([buf[s, r, lanes(256)] for s, r in where], axis=0)
+        k_high, k_low = split(keys)
+        v_high, v_low = split(values)
+        k_high = jnp.concatenate([k_high, k_high], axis=1)
+        k_low = jnp.concatenate([k_low, k_low], axis=1)
+        v_both = jnp.concatenate([v_high, v_low], axis=1)
+        q = q_cat[b, n]
+        dims = (((1,), (1,)), ((), ()))
+        scores = lax.dot_general(q, k_high, dims, preferred_element_type=jnp.float32)
+        scores = scores + lax.dot_general(q, k_low, dims, preferred_element_type=jnp.float32)
+        scores = (scores.reshape(PER_GROUP, BLOCK, 256) + bias[None]).reshape(PER_GROUP * BLOCK, 256)
+        old = top[b, n]
+        new = jnp.maximum(old, jnp.max(scores, axis=1, keepdims=True))
+        weights = jnp.exp2(scores - jnp.concatenate([new, new], axis=1))
+        alpha = jnp.exp2(old - new)
+        top[b, n] = new
+        total[b, n] = total[b, n] * alpha + weights[:, :128] + weights[:, 128:]
+        w_high, w_low = split(weights)
+        o = jnp.dot(w_high, v_both, preferred_element_type=jnp.float32)
+        o = o + jnp.dot(w_low, v_both, preferred_element_type=jnp.float32)
+        acc[b, n] = acc[b, n] * alpha + o[:, :128] + o[:, 128:]
+
+    def turn(t, _):
+        for name, start in STAGES:
+            when((t >= start) & (t < start + CHUNKS), lambda name=name, start=start: stage[name](t - start))
+        when(t == 20, lambda: wait_all((16,)))
+        when(t == 24, lambda: wait_all((4, 256)))
+        half = pick(t, [WORK.get(i, -1) for i in range(TURNS)])
+
+        @pl.when(half >= 0)
+        def _():
+            step(half // 2, half % 2)
         return 0
 
-    lax.fori_loop(0, 12, step, 0)
+    lax.fori_loop(0, TURNS, turn, 0)
 
     for b in range(2):
         for n in range(GROUPS):
@@ -243,10 +258,10 @@
             sent(rule)
         when(z < 7, lambda: sent("2"))
         when(z == 6, lambda: sent("2b"))
-        when(z_plus, lambda: sent("4"))
-        when(z_forward, lambda: sent("4f"))
-        when(z_minus, lambda: sent("4a"))
-        when(y_odd, lambda: sent("256a"))
+        when(k >= back_plus, lambda: sent("4"))
+        when(k < back_relay, lambda: sent("4f"))
+        when(k < back_own, lambda: sent("4a"))
+        when(k < Y_BACK, lambda: sent("256a"))
         return 0
 
     lax.fori_loop(0, CHUNKS, finish, 0)

time: 82.5 us -> 72.2 us (0.88)
  the two profiles are of different devices: /device:TPU:128 before, /device:TPU:2 now
where the time goes in v2:
time: 72.2 us; the launch traced here: 72 us
  Pallas kernels  69.3 us (96%)
  local copies, waits for them, and re-layouts  2.66 us (4%)
    pallas_call x1, Pallas kernels, body(): pl.pallas_call(kernel, out_shape=jax.ShapeDtypeStruct((ROWS, HEADS * FEAT...  69.3 us
    unnamed x1, local copies, waits for them, and re-layouts  2.66 us

profile of v2, /device:TPU:2, one launch (start us, length us, event | category | flops | bytes accessed | tf_op | source)
XLA Modules:
  0.0 72.0 jit_solution(12723843679672338899)
XLA Ops:
  0.0 69.3 %shard_map.46 = f32[256,1536]{1,0:T(8,128)} custom-call(f32[256,1536]{1,0:T(8,128)} %q_ref.1, f32[256,256]{1,0:T(8,128)} %k_ref.1, f32[256,256]{1,0:T(8,128)} %v_ref.1, s32[2,15]{1,0:T(2,128)} %lists_ref.1), custom_call_target="tpu_custom_call" | custom-call | tf_op jit(solution)/shard_map/pallas_call | solution.py:272
  69.3 2.7 %copy.6 = f32[256,1536]{1,0:T(8,128)} copy(f32[256,1536]{1,0:T(8,128)} %shard_map.46) | data formatting | bytes 3145728

commit v3 on v2

--- a/solution.py
+++ b/solution.py
@@ -20,14 +20,14 @@
 Z_BACK = (2, 6, 1, 6, 8, 8, 1, 6)
 Y_BACK = 4
 STAGES = (("8", 0), ("64", 0), ("1", 0), ("own 32", 4), ("32", 8), ("z", 8), ("y", 8), ("2", 8), ("128", 8))
-TURNS = 28
-WORK = {1: 0, 2: 1, 4: 2, 5: 3, **{t: t - 4 for t in range(8, TURNS)}}
+TURNS = 25
+WORK = {t: t - 1 for t in range(1, TURNS)}
 NEG = -1e30
 MESH = pl.DeviceIdType.MESH
 
 STEPS = (
-    (1, (0, 0), (0, 1)), (0, (0, 0), (8, 0)), (0, (1, 0), (1, 1)), (1, (1, 0), (1, 1)), (1, (8, 1), (64, 1)), (0, (64, 0), (128, 0)),
-    (0, (2, 0), (2, 1)), (1, (2, 1), (128, 1)), (0, (32, 0), (16, 0)), (1, (32, 1), (16, 1)), (0, (4, 0), (256, 0)), (1, (4, 1), (256, 1)),
+    (1, (0, 0), (0, 1)), (0, (0, 0), (8, 0)), (0, (1, 0), (64, 0)), (1, (1, 0), (1, 1)), (1, (8, 1), (64, 1)), (0, (1, 1), (128, 0)),
+    (0, (2, 0), (32, 0)), (1, (2, 1), (128, 1)), (0, (2, 1), (16, 0)), (1, (32, 1), (16, 1)), (0, (4, 0), (256, 0)), (1, (4, 1), (256, 1)),
 )
 
 
@@ -180,12 +180,12 @@
     col = lax.broadcasted_iota(jnp.int32, (BLOCK, 256), 1)
     row = lax.broadcasted_iota(jnp.int32, (BLOCK, 256), 0)
 
-    def wait_all(offsets):
+    def wait_all(offsets, start=0, stop=CHUNKS):
         def body(k, _):
             for o in offsets:
                 arrive(SLOT[o], k)
             return 0
-        lax.fori_loop(0, CHUNKS, body, 0)
+        lax.fori_loop(start, stop, body, 0)
 
     def step(i, n):
         b = pick(i, [s[0] for s in STEPS])
@@ -204,6 +204,7 @@
             hit = hit | (target[0:8] == lists_ref[b, m])
         bias8 = jnp.where(hit & (target[0:8] >= 0), jnp.float32(0), jnp.float32(NEG))
         bias = jnp.where((away > 0) | (col % BLOCK <= row), jnp.broadcast_to(bias8[0:1], (BLOCK, 256)), jnp.float32(NEG))
+
         def lanes(start):
             return pl.ds(pl.multiple_of(start + n * FEATURES, FEATURES), FEATURES)
 
@@ -211,13 +212,12 @@
         values = jnp.concatenate([buf[s, r, lanes(256)] for s, r in where], axis=0)
         k_high, k_low = split(keys)
         v_high, v_low = split(values)
-        k_high = jnp.concatenate([k_high, k_high], axis=1)
-        k_low = jnp.concatenate([k_low, k_low], axis=1)
+        k_cat = jnp.concatenate([k_high, k_high, k_low, k_low], axis=1)
         v_both = jnp.concatenate([v_high, v_low], axis=1)
+        v_cat = jnp.concatenate([v_both, v_both], axis=0)
+        dims = (((1,), (1,)), ((), ()))
         q = q_cat[b, n]
-        dims = (((1,), (1,)), ((), ()))
-        scores = lax.dot_general(q, k_high, dims, preferred_element_type=jnp.float32)
-        scores = scores + lax.dot_general(q, k_low, dims, preferred_element_type=jnp.float32)
+        scores = lax.dot_general(jnp.concatenate([q, q], axis=1), k_cat, dims, preferred_element_type=jnp.float32)
         scores = (scores.reshape(PER_GROUP, BLOCK, 256) + bias[None]).reshape(PER_GROUP * BLOCK, 256)
         old = top[b, n]
         new = jnp.maximum(old, jnp.max(scores, axis=1, keepdims=True))
@@ -226,15 +226,15 @@
         top[b, n] = new
         total[b, n] = total[b, n] * alpha + weights[:, :128] + weights[:, 128:]
         w_high, w_low = split(weights)
-        o = jnp.dot(w_high, v_both, preferred_element_type=jnp.float32)
-        o = o + jnp.dot(w_low, v_both, preferred_element_type=jnp.float32)
+        o = jnp.dot(jnp.concatenate([w_high, w_low], axis=1), v_cat, preferred_element_type=jnp.float32)
         acc[b, n] = acc[b, n] * alpha + o[:, :128] + o[:, 128:]
 
     def turn(t, _):
         for name, start in STAGES:
             when((t >= start) & (t < start + CHUNKS), lambda name=name, start=start: stage[name](t - start))
-        when(t == 20, lambda: wait_all((16,)))
-        when(t == 24, lambda: wait_all((4, 256)))
+        when(t == 17, lambda: wait_all((16,)))
+        when(t == 21, lambda: wait_all((4, 256), 0, CHUNKS // 2))
+        when(t == 23, lambda: wait_all((4, 256), CHUNKS // 2))
         half = pick(t, [WORK.get(i, -1) for i in range(TURNS)])
 
         @pl.when(half >= 0)
@@ -246,7 +246,7 @@
 
     for b in range(2):
         for n in range(GROUPS):
-            out = acc[b, n] / jnp.sum(total[b, n], axis=1, keepdims=True)
+            out = acc[b, n] * (1 / jnp.sum(total[b, n], axis=1, keepdims=True))
             for r in range(PER_GROUP):
                 m = n * PER_GROUP + r
                 out_ref[b * BLOCK:(b + 1) * BLOCK, m * FEATURES:(m + 1) * FEATURES] = out[r * BLOCK:(r + 1) * BLOCK]
@@ -271,7 +271,7 @@
     pair = (2, GROUPS, PER_GROUP * BLOCK)
     return pl.pallas_call(
         kernel,
-        out_shape=jax.ShapeDtypeStruct((ROWS, HEADS * FEATURES), jnp.float32),
+        out_shape=pltpu.VMEM((ROWS, HEADS * FEATURES), jnp.float32),
         in_specs=[pl.BlockSpec(memory_space=pl.ANY)] * 3 + [pl.BlockSpec(memory_space=pltpu.SMEM)],
         out_specs=pl.BlockSpec(memory_space=pltpu.VMEM),
         scratch_shapes=[

time: 72.2 us -> 65.8 us (0.911)
  the two profiles are of different devices: /device:TPU:2 before, /device:TPU:4 now
where the time goes in v3:
time: 65.8 us; the launch traced here: 65.6 us
  Pallas kernels  64.5 us (98%)
  local copies, waits for them, and re-layouts  1.15 us (2%)
    pallas_call x1, Pallas kernels, body(): pl.pallas_call(kernel, out_shape=pltpu.VMEM((ROWS, HEADS * FEATURES), jnp...  64.5 us

profile of v3, /device:TPU:4, one launch (start us, length us, event | category | flops | bytes accessed | tf_op | source)
XLA Modules:
  0.0 65.6 jit_solution(18377780852034281405)
XLA Ops:
  0.0 64.5 %shard_map.46 = f32[256,1536]{1,0:T(8,128)S(1)} custom-call(f32[256,1536]{1,0:T(8,128)} %q_ref.1, f32[256,256]{1,0:T(8,128)} %k_ref.1, f32[256,256]{1,0:T(8,128)} %v_ref.1, s32[2,15]{1,0:T(2,128)} %lists_ref.1), custom_call_target="tpu_custom_call" | custom-call | tf_op jit(solution)/shard_map/pallas_call | solution.py:272
  64.5 1.1 %copy.6 = f32[256,1536]{1,0:T(8,128)} copy(f32[256,1536]{1,0:T(8,128)S(1)} %shard_map.46) | data formatting | bytes 3145728

commit v4 on v3

--- a/solution.py
+++ b/solution.py
@@ -17,11 +17,11 @@
 RULES = ("1", "2", "2b", "4", "4f", "4a", "8", "16", "32", "64", "128", "256", "256a")
 CHUNKS = 8
 CHUNK = ROWS // CHUNKS
-Z_BACK = (2, 6, 1, 6, 8, 8, 1, 6)
-Y_BACK = 4
-STAGES = (("8", 0), ("64", 0), ("1", 0), ("own 32", 4), ("32", 8), ("z", 8), ("y", 8), ("2", 8), ("128", 8))
-TURNS = 25
-WORK = {t: t - 1 for t in range(1, TURNS)}
+Z_BACK = (4, 6, 2, 8, 8, 8, 2, 6)
+Y_BACK = 5
+STAGES = (("8", 0), ("64", 0), ("1", 0), ("own 32", 1), ("32", 8), ("y", 8), ("128", 8), ("z", 8), ("2", 8))
+TURNS = 21
+WORK = {2: 0, 4: 1, 6: 2, 8: 3, 10: 4, 12: 5, 14: 6, **{t: t - 9 for t in range(16, TURNS)}}
 NEG = -1e30
 MESH = pl.DeviceIdType.MESH
 
@@ -114,8 +114,8 @@
         return go
 
     own_32 = own("32", SLOT[32], t32, lambda k: no(g1))
-    for go in (own("64", SLOT[64], y1), own("8", SLOT[8], t8, lambda k: no(y8)), own("1", SLOT[1], t1, lambda k: z < 7),
-               own("4a", RELAY_Z, tzm2, lambda k: (k < back_own) & no(z_high)),
+    for go in (own("1", SLOT[1], t1, lambda k: z < 7), own("4a", RELAY_Z, tzm2, lambda k: (k < back_own) & no(z_high)),
+               own("8", SLOT[8], t8, lambda k: no(y8)), own("64", SLOT[64], y1),
                own("16", SLOT[16], t16, lambda k: c == 0), own("256a", RELAY_Y, ym2, lambda k: k < Y_BACK)):
         def first(k, _, go=go):
             go(k)
@@ -187,7 +187,7 @@
             return 0
         lax.fori_loop(start, stop, body, 0)
 
-    def step(i, n):
+    def step(i):
         b = pick(i, [s[0] for s in STEPS])
         where = []
         distance = []
@@ -205,51 +205,33 @@
         bias8 = jnp.where(hit & (target[0:8] >= 0), jnp.float32(0), jnp.float32(NEG))
         bias = jnp.where((away > 0) | (col % BLOCK <= row), jnp.broadcast_to(bias8[0:1], (BLOCK, 256)), jnp.float32(NEG))
 
-        def lanes(start):
-            return pl.ds(pl.multiple_of(start + n * FEATURES, FEATURES), FEATURES)
-
-        keys = jnp.concatenate([buf[s, r, lanes(0)] for s, r in where], axis=0)
-        values = jnp.concatenate([buf[s, r, lanes(256)] for s, r in where], axis=0)
-        k_high, k_low = split(keys)
-        v_high, v_low = split(values)
-        k_cat = jnp.concatenate([k_high, k_high, k_low, k_low], axis=1)
-        v_both = jnp.concatenate([v_high, v_low], axis=1)
-        v_cat = jnp.concatenate([v_both, v_both], axis=0)
-        dims = (((1,), (1,)), ((), ()))
-        q = q_cat[b, n]
-        scores = lax.dot_general(jnp.concatenate([q, q], axis=1), k_cat, dims, preferred_element_type=jnp.float32)
-        scores = (scores.reshape(PER_GROUP, BLOCK, 256) + bias[None]).reshape(PER_GROUP * BLOCK, 256)
-        old = top[b, n]
-        new = jnp.maximum(old, jnp.max(scores, axis=1, keepdims=True))
-        weights = jnp.exp2(scores - jnp.concatenate([new, new], axis=1))
-        alpha = jnp.exp2(old - new)
-        top[b, n] = new
-        total[b, n] = total[b, n] * alpha + weights[:, :128] + weights[:, 128:]
-        w_high, w_low = split(weights)
-        o = jnp.dot(jnp.concatenate([w_high, w_low], axis=1), v_cat, preferred_element_type=jnp.float32)
-        acc[b, n] = acc[b, n] * alpha + o[:, :128] + o[:, 128:]
-
-    def turn(t, _):
-        for name, start in STAGES:
-            when((t >= start) & (t < start + CHUNKS), lambda name=name, start=start: stage[name](t - start))
-        when(t == 17, lambda: wait_all((16,)))
-        when(t == 21, lambda: wait_all((4, 256), 0, CHUNKS // 2))
-        when(t == 23, lambda: wait_all((4, 256), CHUNKS // 2))
-        half = pick(t, [WORK.get(i, -1) for i in range(TURNS)])
-
-        @pl.when(half >= 0)
-        def _():
-            step(half // 2, half % 2)
-        return 0
-
-    lax.fori_loop(0, TURNS, turn, 0)
-
-    for b in range(2):
+        ahead = []
         for n in range(GROUPS):
-            out = acc[b, n] * (1 / jnp.sum(total[b, n], axis=1, keepdims=True))
-            for r in range(PER_GROUP):
-                m = n * PER_GROUP + r
-                out_ref[b * BLOCK:(b + 1) * BLOCK, m * FEATURES:(m + 1) * FEATURES] = out[r * BLOCK:(r + 1) * BLOCK]
+            def lanes(start, n=n):
+                return pl.ds(start + n * FEATURES, FEATURES)
+
+            keys = jnp.concatenate([buf[s, r, lanes(0)] for s, r in where], axis=0)
+            values = jnp.concatenate([buf[s, r, lanes(256)] for s, r in where], axis=0)
+            k_high, k_low = split(keys)
+            v_high, v_low = split(values)
+            k_cat = jnp.concatenate([k_high, k_high, k_low, k_low], axis=1)
+            v_both = jnp.concatenate([v_high, v_low], axis=1)
+            v_cat = jnp.concatenate([v_both, v_both], axis=0)
+            dims = (((1,), (1,)), ((), ()))
+            q = q_cat[b, n]
+            scores = lax.dot_general(jnp.concatenate([q, q], axis=1), k_cat, dims, preferred_element_type=jnp.float32)
+            scores = (scores.reshape(PER_GROUP, BLOCK, 256) + bias[None]).reshape(PER_GROUP * BLOCK, 256)
+            ahead.append((scores, v_cat))
+        for n, (scores, v_cat) in enumerate(ahead):
+            old = top[b, n]
+            new = jnp.maximum(old, jnp.max(scores, axis=1, keepdims=True))
+            weights = jnp.exp2(scores - jnp.concatenate([new, new], axis=1))
+            alpha = jnp.exp2(old - new)
+            top[b, n] = new
+            total[b, n] = total[b, n] * alpha + weights[:, :128] + weights[:, 128:]
+            w_high, w_low = split(weights)
+            o = jnp.dot(jnp.concatenate([w_high, w_low], axis=1), v_cat, preferred_element_type=jnp.float32)
+            acc[b, n] = acc[b, n] * alpha + o[:, :128] + o[:, 128:]
 
     def finish(k, _):
         def sent(rule):
@@ -264,7 +246,32 @@
         when(k < Y_BACK, lambda: sent("256a"))
         return 0
 
-    lax.fori_loop(0, CHUNKS, finish, 0)
+    def turn(t, _):
+        for name, start in STAGES:
+            when((t >= start) & (t < start + CHUNKS), lambda name=name, start=start: stage[name](t - start))
+        when(t == 17, lambda: wait_all((16,)))
+        when(t == 19, lambda: wait_all((4, 256), 0, CHUNKS // 2))
+
+        @pl.when(t == 20)
+        def _():
+            lax.fori_loop(0, CHUNKS, finish, 0)
+            wait_all((4, 256), CHUNKS // 2)
+
+        half = pick(t, [WORK.get(i, -1) for i in range(TURNS)])
+
+        @pl.when(half >= 0)
+        def _():
+            step(half)
+        return 0
+
+    lax.fori_loop(0, TURNS, turn, 0)
+
+    for b in range(2):
+        for n in range(GROUPS):
+            out = acc[b, n] * (1 / jnp.sum(total[b, n], axis=1, keepdims=True))
+            for r in range(PER_GROUP):
+                m = n * PER_GROUP + r
+                out_ref[b * BLOCK:(b + 1) * BLOCK, m * FEATURES:(m + 1) * FEATURES] = out[r * BLOCK:(r + 1) * BLOCK]
 
 
 def body(query_matrix, key_matrix, value_matrix, block_lists):

time: 65.8 us -> 61 us (0.927)
  the two profiles are of different devices: /device:TPU:4 before, /device:TPU:16 now
where the time goes in v4:
time: 61 us; the launch traced here: 60.8 us
  Pallas kernels  59.7 us (98%)
  local copies, waits for them, and re-layouts  1.15 us (2%)
    pallas_call x1, Pallas kernels, body(): pl.pallas_call(kernel, out_shape=pltpu.VMEM((ROWS, HEADS * FEATURES), jnp...  59.7 us

profile of v4, /device:TPU:16, one launch (start us, length us, event | category | flops | bytes accessed | tf_op | source)
XLA Modules:
  0.0 60.8 jit_solution(16893674089467702474)
XLA Ops:
  0.0 59.7 %shard_map.46 = f32[256,1536]{1,0:T(8,128)S(1)} custom-call(f32[256,1536]{1,0:T(8,128)} %q_ref.1, f32[256,256]{1,0:T(8,128)} %k_ref.1, f32[256,256]{1,0:T(8,128)} %v_ref.1, s32[2,15]{1,0:T(2,128)} %lists_ref.1), custom_call_target="tpu_custom_call" | custom-call | tf_op jit(solution)/shard_map/pallas_call | solution.py:279
  59.7 1.1 %copy.6 = f32[256,1536]{1,0:T(8,128)} copy(f32[256,1536]{1,0:T(8,128)S(1)} %shard_map.46) | data formatting | bytes 3145728

commit v5 on v4

--- a/solution.py
+++ b/solution.py
@@ -19,9 +19,9 @@
 CHUNK = ROWS // CHUNKS
 Z_BACK = (4, 6, 2, 8, 8, 8, 2, 6)
 Y_BACK = 5
-STAGES = (("8", 0), ("64", 0), ("1", 0), ("own 32", 1), ("32", 8), ("y", 8), ("128", 8), ("z", 8), ("2", 8))
+STAGES = (("8", 1), ("64", 1), ("1", 1), ("own 32", 2), ("32", 9), ("y", 9), ("128", 9), ("z", 9), ("2", 9))
 TURNS = 21
-WORK = {2: 0, 4: 1, 6: 2, 8: 3, 10: 4, 12: 5, 14: 6, **{t: t - 9 for t in range(16, TURNS)}}
+WORK = {0: 0, 4: 1, 6: 2, 8: 3, 10: 4, 12: 5, 14: 6, **{t: t - 9 for t in range(16, TURNS)}}
 NEG = -1e30
 MESH = pl.DeviceIdType.MESH
 
@@ -246,6 +246,13 @@
         when(k < Y_BACK, lambda: sent("256a"))
         return 0
 
+    def settle(b):
+        for n in range(GROUPS):
+            out = acc[b, n] * (1 / jnp.sum(total[b, n], axis=1, keepdims=True))
+            for r in range(PER_GROUP):
+                m = n * PER_GROUP + r
+                out_ref[b * BLOCK:(b + 1) * BLOCK, m * FEATURES:(m + 1) * FEATURES] = out[r * BLOCK:(r + 1) * BLOCK]
+
     def turn(t, _):
         for name, start in STAGES:
             when((t >= start) & (t < start + CHUNKS), lambda name=name, start=start: stage[name](t - start))
@@ -254,6 +261,7 @@
 
         @pl.when(t == 20)
         def _():
+            settle(0)
             lax.fori_loop(0, CHUNKS, finish, 0)
             wait_all((4, 256), CHUNKS // 2)
 
@@ -266,12 +274,7 @@
 
     lax.fori_loop(0, TURNS, turn, 0)
 
-    for b in range(2):
-        for n in range(GROUPS):
-            out = acc[b, n] * (1 / jnp.sum(total[b, n], axis=1, keepdims=True))
-            for r in range(PER_GROUP):
-                m = n * PER_GROUP + r
-                out_ref[b * BLOCK:(b + 1) * BLOCK, m * FEATURES:(m + 1) * FEATURES] = out[r * BLOCK:(r + 1) * BLOCK]
+    settle(1)
 
 
 def body(query_matrix, key_matrix, value_matrix, block_lists):

time: 61 us -> 60.5 us (level)
  the two profiles are of different devices: /device:TPU:16 before, /device:TPU:128 now
where the time goes in v5:
time: 60.5 us; the launch traced here: 60.3 us
  Pallas kernels  59.2 us (98%)
  local copies, waits for them, and re-layouts  1.15 us (2%)
    pallas_call x1, Pallas kernels, body(): pl.pallas_call(kernel, out_shape=pltpu.VMEM((ROWS, HEADS * FEATURES), jnp...  59.2 us

profile of v5, /device:TPU:128, one launch (start us, length us, event | category | flops | bytes accessed | tf_op | source)
XLA Modules:
  0.0 60.3 jit_solution(14697771350073181596)
XLA Ops:
  0.0 59.2 %shard_map.46 = f32[256,1536]{1,0:T(8,128)S(1)} custom-call(f32[256,1536]{1,0:T(8,128)} %q_ref.1, f32[256,256]{1,0:T(8,128)} %k_ref.1, f32[256,256]{1,0:T(8,128)} %v_ref.1, s32[2,15]{1,0:T(2,128)} %lists_ref.1), custom_call_target="tpu_custom_call" | custom-call | tf_op jit(solution)/shard_map/pallas_call | solution.py:282
  59.2 1.1 %copy.6 = f32[256,1536]{1,0:T(8,128)} copy(f32[256,1536]{1,0:T(8,128)S(1)} %shard_map.46) | data formatting | bytes 3145728

commit v6 on v5

--- a/solution.py
+++ b/solution.py
@@ -19,7 +19,7 @@
 CHUNK = ROWS // CHUNKS
 Z_BACK = (4, 6, 2, 8, 8, 8, 2, 6)
 Y_BACK = 5
-STAGES = (("8", 1), ("64", 1), ("1", 1), ("own 32", 2), ("32", 9), ("y", 9), ("128", 9), ("z", 9), ("2", 9))
+STAGES = (("64", 1), ("8", 1), ("1", 1), ("own 32", 2), ("32", 9), ("y", 9), ("128", 9), ("z", 9), ("2", 9))
 TURNS = 21
 WORK = {0: 0, 4: 1, 6: 2, 8: 3, 10: 4, 12: 5, 14: 6, **{t: t - 9 for t in range(16, TURNS)}}
 NEG = -1e30

time: 60.5 us -> 60.6 us (level)
  no operation moved by 1% of the time
where the time goes in v6:
time: 60.6 us; the launch traced here: 60.4 us
  Pallas kernels  59.3 us (98%)
  local copies, waits for them, and re-layouts  1.15 us (2%)
    pallas_call x1, Pallas kernels, body(): pl.pallas_call(kernel, out_shape=pltpu.VMEM((ROWS, HEADS * FEATURES), jnp...  59.3 us

profile of v6, /device:TPU:128, one launch (start us, length us, event | category | flops | bytes accessed | tf_op | source)
XLA Modules:
  0.0 60.4 jit_solution(5751574624437860735)
XLA Ops:
  0.0 59.3 %shard_map.46 = f32[256,1536]{1,0:T(8,128)S(1)} custom-call(f32[256,1536]{1,0:T(8,128)} %q_ref.1, f32[256,256]{1,0:T(8,128)} %k_ref.1, f32[256,256]{1,0:T(8,128)} %v_ref.1, s32[2,15]{1,0:T(2,128)} %lists_ref.1), custom_call_target="tpu_custom_call" | custom-call | tf_op jit(solution)/shard_map/pallas_call | solution.py:282
  59.3 1.1 %copy.6 = f32[256,1536]{1,0:T(8,128)} copy(f32[256,1536]{1,0:T(8,128)S(1)} %shard_map.46) | data formatting | bytes 3145728
